TPU v7x, 32 devices: a whole 2x2x4 slice. The times are simulated.
32 devices in a mesh: groups: 2 (over y), tp: 4 (over z), dp: 4 (over x, core).
Axes of the slice: x: 2, y: 2, z: 4, core: 2. Of those that a mesh axis runs over, the one named last changes fastest.
Arguments:
- tokens: bfloat16 [256, 7168], P(('groups', 'tp'), 'dp'), parts along dimension 0, may hold values from -6 to 6
- counts: int32 [8], P(('groups', 'tp')), parts along dimension 0, may hold values from 0 to 32, as said below
- gate_weight: bfloat16 [7168, 18432], P('dp', 'tp'), may hold values from -0.0625 to 0.0625
- up_weight: bfloat16 [7168, 18432], P('dp', 'tp'), may hold values from -0.0625 to 0.0625
- down_weight: bfloat16 [18432, 7168], P('tp', 'dp'), may hold values from -0.046875 to 0.046875
Outputs:
- mixed: bfloat16 [256, 7168], P(('groups', 'tp'), 'dp'), parts along dimension 0
There are 2 independent parts, one for each index of `groups`. A program takes and returns all parts, laid end to end along the dimension named above; an argument that names none is the same for every part. Nothing has to cross between parts.
Inputs may be any that keep to these rules, and one draw needn't show every extreme that they name: `counts`: some attention rank has all 32 slots live in every draw.
All inputs are finite; a program needn't handle non-finite values.
Results may differ from a plain program's by a relative error of at most 0.005.
Values may be sent and summed in bfloat16 or wider, within the bound.
A program may use at most 128 MiB of HBM per device.

v0:
```python
import jax
import jax.numpy as jnp
from jax import lax
from jax.sharding import PartitionSpec as P


def on_device(tokens, counts, gate_weight, up_weight, down_weight):
    width = gate_weight.shape[1]
    gathered = lax.all_gather(tokens, "tp", axis=0, tiled=True)
    gate_part = jnp.dot(gathered, gate_weight, preferred_element_type=jnp.float32)
    up_part = jnp.dot(gathered, up_weight, preferred_element_type=jnp.float32)
    both = jnp.concatenate([gate_part, up_part], axis=1)
    shared = lax.psum_scatter(both, "dp", scatter_dimension=0, tiled=True)
    active = (jax.nn.silu(shared[:, :width]) * shared[:, width:]).astype(jnp.bfloat16)
    hidden = lax.all_gather(active, "dp", axis=0, tiled=True)
    product = lax.psum_scatter(
        jnp.dot(hidden, down_weight, preferred_element_type=jnp.float32),
        "tp",
        scatter_dimension=0,
        tiled=True,
    )
    live = jnp.arange(tokens.shape[0], dtype=jnp.int32) < counts[0]
    return jnp.where(live[:, None], product, jnp.float32(0.0)).astype(jnp.bfloat16)


def solution(mesh):
    in_specs = (
        P(("groups", "tp"), "dp"),
        P(("groups", "tp")),
        P("dp", "tp"),
        P("dp", "tp"),
        P("tp", "dp"),
    )
    out_specs = P(("groups", "tp"), "dp")
    return jax.shard_map(
        on_device, mesh=mesh, in_specs=in_specs, out_specs=out_specs, check_vma=False
    )
```

profile of v0, /device:TPU:0, one launch (start us, length us, event | category | flops | bytes accessed | tf_op | source)
XLA Modules:
  0.0 151.0 jit_solution(8247720332029724139)
XLA Ops:
  6.5 0.0 reduce-scatter.3.cloned.1.call-start
  6.5 17.0 %all_gather.6 = bf16[128,1792]{1,0:T(8,128)(2,1)S(1)} all-gather(bf16[32,1792]{1,0:T(8,128)(2,1)} %param.5), channel_id=1, replica_groups=mesh['groups'=2,'tp'=4,'dp'=4] {'tp'}, dimensions={0}, use_global_device_ids=true | all-gather | bytes 573440 | tf_op jit(solution)/shard_map/all_gather | solution.py:9
  23.5 0.0 copy-start
  23.5 8.2 %fusion.1 = f32[128,4608]{1,0:T(8,128)S(1)} fusion(bf16[128,1792]{1,0:T(8,128)(2,1)S(1)} %all_gather.6, bf16[1792,4608]{1,0:T(8,128)(2,1)} %param.7), kind=kOutput, calls=%fused_computation.5 | convolution fusion | flops 2113929216 | bytes 19333120 | tf_op jit(solution)/shard_map/dot_general | solution.py:10
  31.7 2.2 %copy-done = bf16[1792,4608]{1,0:T(8,128)(2,1)S(1)} copy-done((bf16[1792,4608]{1,0:T(8,128)(2,1)S(1)}, bf16[1792,4608]{1,0:T(8,128)(2,1)}, u32[]{:S(2)}) %copy-start) | copy-done | bytes 16515096
  33.9 2.3 %fusion.2 = f32[128,4608]{1,0:T(8,128)S(1)} fusion(bf16[128,1792]{1,0:T(8,128)(2,1)S(1)} %all_gather.6, bf16[1792,4608]{1,0:T(8,128)(2,1)S(1)} %copy-done), kind=kOutput, calls=%fused_computation.6 | convolution fusion | flops 2113929216 | bytes 19333120 | tf_op jit(solution)/shard_map/dot_general | solution.py:11
  36.2 2.4 %pad_maximum_fusion = f32[128,9216]{1,0:T(8,128)} fusion(f32[128,4608]{1,0:T(8,128)S(1)} %fusion.2, f32[128,4608]{1,0:T(8,128)S(1)} %fusion.1), kind=kLoop, calls=%fused_computation | loop fusion | flops 1179648 | bytes 9437184 | tf_op jit(solution)/shard_map/concatenate | solution.py:12
  38.7 0.0 reduce-scatter.3.cloned.1.call-update
  38.7 0.0 all-gather.2.cloned.1.call-start
  38.7 49.7 %reduce-scatter.3.cloned.1.call-done = f32[32,9216]{1,0:T(8,128)} async-done(((f32[128,9216]{1,0:T(8,128)}), f32[32,9216]{1,0:T(8,128)}) %reduce-scatter.3.cloned.1.call-update) | async-done | bytes 1179664 | tf_op jit(solution)/shard_map/reduce_scatter | solution.py:13
  88.4 2.1 %fusion = bf16[32,4608]{1,0:T(8,128)(2,1)} fusion(f32[32,9216]{1,0:T(8,128)} %reduce-scatter.3.cloned.1.call-done), kind=kLoop, calls=%fused_computation.2 | loop fusion | flops 884736 | bytes 1474560 | tf_op jit(solution)/shard_map/convert_element_type | solution.py:14
  90.6 0.0 all-gather.2.cloned.1.call-update
  90.6 0.0 reduce-scatter.5.cloned.1.call-start
  90.7 17.6 %all-gather.2.cloned.1.call-done = bf16[128,4608]{1,0:T(8,128)(2,1)} async-done(((bf16[32,4608]{1,0:T(8,128)(2,1)}), bf16[128,4608]{1,0:T(8,128)(2,1)}) %all-gather.2.cloned.1.call-update) | async-done | bytes 1179664 | tf_op jit(solution)/shard_map/all_gather | solution.py:15
  108.2 9.3 %fusion.3 = f32[128,1792]{1,0:T(8,128)} fusion(bf16[128,4608]{1,0:T(8,128)(2,1)} %all-gather.2.cloned.1.call-done, bf16[4608,1792]{1,0:T(8,128)(2,1)} %param.9), kind=kOutput, calls=%fused_computation.7 | convolution fusion | flops 2113929216 | bytes 18612224 | tf_op jit(solution)/shard_map/dot_general | solution.py:17
  117.5 0.0 reduce-scatter.5.cloned.1.call-update
  118.2 24.6 %reduce-scatter.5.cloned.1.call-done = f32[32,1792]{1,0:T(8,128)} async-done(((f32[128,1792]{1,0:T(8,128)}), f32[32,1792]{1,0:T(8,128)}) %reduce-scatter.5.cloned.1.call-update) | async-done | bytes 229392 | tf_op jit(solution)/shard_map/reduce_scatter | solution.py:16
  142.8 1.7 %select_convert_fusion = bf16[32,1792]{1,0:T(8,128)(2,1)} fusion(f32[32,1792]{1,0:T(8,128)} %reduce-scatter.5.cloned.1.call-done, pred[32]{0:T(512)(128)(4,1)S(1)} %iota_compare_fusion), kind=kLoop, calls=%fused_computation.3 | loop fusion | flops 57344 | bytes 344096 | tf_op jit(solution)/shard_map/convert_element_type | solution.py:23
  (1 shorter events, 0.0 us)
Async XLA Ops:
  6.5 81.9 %reduce-scatter.3.cloned.1.call-start = ((), (), s32[]{:S(2)}) async-start(), calls=%async_computation.2 | async-start | bytes 5898240 | tf_op jit(solution)/shard_map/reduce_scatter | solution.py:13
  23.5 10.4 %copy-start = (bf16[1792,4608]{1,0:T(8,128)(2,1)S(1)}, bf16[1792,4608]{1,0:T(8,128)(2,1)}, u32[]{:S(2)}) copy-start(bf16[1792,4608]{1,0:T(8,128)(2,1)} %param.8) | copy-start | bytes 49545220
  38.7 69.5 %all-gather.2.cloned.1.call-start = ((), (), s32[]{:S(2)}) async-start(), calls=%async_computation.3 | async-start | bytes 1474560 | tf_op jit(solution)/shard_map/all_gather | solution.py:15
  90.6 52.2 %reduce-scatter.5.cloned.1.call-start = ((), (), s32[]{:S(2)}) async-start(), calls=%async_computation.4 | async-start | bytes 1146880 | tf_op jit(solution)/shard_map/reduce_scatter | solution.py:16
Sparse Core Ops, SparseCore 0:
  38.8 49.5 reduce-scatter.2
  90.7 17.4 all-gather.1
  117.7 25.0 reduce-scatter.4
where the time goes:
time: 151 us
  waiting for transfers between devices  91.9 us (61%)
  matrix products  19.8 us (13%)
  blocking collectives  17 us (11%)
  between operations  13.8 us (9%)
  other arithmetic  6.25 us (4%)
  local copies, waits for them, and re-layouts  2.23 us (1%)
    reduce_scatter x1, waiting for transfers between devices, on_device(): shared = lax.psum_scatter(both, 'dp', scatter_dimension=0, tiled=True)  49.7 us
    reduce_scatter x1, waiting for transfers between devices, on_device(): lax.psum_scatter(jnp.dot(hidden, down_weight, preferred_element_type=jnp....  24.6 us
    all_gather x1, waiting for transfers between devices, on_device(): hidden = lax.all_gather(active, 'dp', axis=0, tiled=True)  17.6 us
    all_gather x1, blocking collectives, on_device(): gathered = lax.all_gather(tokens, 'tp', axis=0, tiled=True)  17 us
    dot_general x1, matrix products, on_device(): jnp.dot(hidden, down_weight, preferred_element_type=jnp.float32)  9.33 us
    dot_general x1, matrix products, on_device(): jnp.dot(gathered, gate_weight, preferred_element_type=jnp.float32)  8.15 us
  transfers between devices with their start and end apart: 3, of which 3 were waited for; matrix products, arithmetic and copies ran while one was open for 0% of the time, Pallas kernels for 0%

commit v1 on v0

v1 whole, which is shorter than its diff:
```python
import functools

import jax
import jax.numpy as jnp
from jax import lax
from jax.experimental import pallas as pl
from jax.experimental.pallas import tpu as pltpu
from jax.sharding import PartitionSpec as P

MESH = pl.DeviceIdType.MESH
SLOTS = 3


def chunk_of(units):
    for width in (512, 384, 256, 128):
        if units % width == 0:
            return width
    return units


def kernel(
    n_tp, n_dp, n, width,
    tokens, gate_w, up_w, down_w, out,
    rows_all, gate_v, up_v, down_v, part, core_in, own, x_out, x_in, hidden, product, z_out, z_in,
    tok_local, tok_s, tok_r, gate_s, up_s, down_s, core_s, core_r, x_s, x_r,
    ag_s, ag_r, sib_s, sib_r, fwd_s, fwd_r, z_s, z_r,
):
    rank = lax.axis_index("tp")
    dp = lax.axis_index("dp")
    n_x = n_dp // 2
    x, core = lax.div(dp, 2), lax.rem(dp, 2)
    sibling = x * 2 + 1 - core
    slots = tokens.shape[0]
    share = slots * n_tp // n_dp

    def x_peer(d):
        return lax.rem(x + d, n_x) * 2 + core

    def block(index, size):
        return pl.ds(pl.multiple_of(index * size, size), size)

    def weight_copies(k):
        columns = pl.ds(pl.multiple_of(k * width, width), width) if n > 1 else pl.ds(0, width)
        return (
            pltpu.make_async_copy(gate_w.at[:, columns], gate_v.at[k], gate_s.at[k]),
            pltpu.make_async_copy(up_w.at[:, columns], up_v.at[k], up_s.at[k]),
        )

    def down_copy(k):
        rows = pl.ds(pl.multiple_of(k * width, width), width) if n > 1 else pl.ds(0, width)
        return pltpu.make_async_copy(down_w.at[rows, :], down_v.at[k], down_s.at[k])

    def token_copy(d):
        return pltpu.make_async_remote_copy(
            src_ref=tokens, dst_ref=rows_all.at[block(rank, slots)],
            send_sem=tok_s.at[d - 1], recv_sem=tok_r.at[d - 1],
            device_id={"tp": lax.rem(rank + d, n_tp)}, device_id_type=MESH,
        )

    def token_arrival(d):
        return pltpu.make_async_remote_copy(
            src_ref=tokens, dst_ref=rows_all.at[block(lax.rem(rank + n_tp - d, n_tp), slots)],
            send_sem=tok_s.at[d - 1], recv_sem=tok_r.at[d - 1],
            device_id={"tp": lax.rem(rank + d, n_tp)}, device_id_type=MESH,
        )

    def core_copy(k, i):
        return pltpu.make_async_remote_copy(
            src_ref=part.at[lax.rem(k, SLOTS), :, block(i * 2 + 1 - core, share), :],
            dst_ref=core_in.at[k, i],
            send_sem=core_s.at[k, i], recv_sem=core_r.at[k, i],
            device_id={"dp": sibling}, device_id_type=MESH,
        )

    def x_copy(k, d):
        return pltpu.make_async_remote_copy(
            src_ref=x_out.at[k, d - 1], dst_ref=x_in.at[k, d - 1],
            send_sem=x_s.at[k, d - 1], recv_sem=x_r.at[k, d - 1],
            device_id={"dp": x_peer(d)}, device_id_type=MESH,
        )

    def hidden_copy(k, owner, target, send, recv):
        ref = hidden.at[k, block(owner, share), :]
        return pltpu.make_async_remote_copy(
            src_ref=ref, dst_ref=ref, send_sem=send, recv_sem=recv,
            device_id={"dp": target}, device_id_type=MESH,
        )

    def ag_copy(k, d):
        return hidden_copy(k, dp, x_peer(d), ag_s.at[k, d - 1], ag_r.at[k, d - 1])

    def ag_arrival(k, d):
        return hidden_copy(k, x_peer(n_x - d), x_peer(d), ag_s.at[k, d - 1], ag_r.at[k, d - 1])

    def sib_copy(k):
        return hidden_copy(k, dp, sibling, sib_s.at[k], sib_r.at[k])

    def sib_arrival(k):
        return hidden_copy(k, sibling, sibling, sib_s.at[k], sib_r.at[k])

    def fwd_copy(k, d):
        return hidden_copy(k, x_peer(n_x - d), sibling, fwd_s.at[k, d - 1], fwd_r.at[k, d - 1])

    def fwd_arrival(k, d):
        owner = lax.rem(x + n_x - d, n_x) * 2 + 1 - core
        return hidden_copy(k, owner, sibling, fwd_s.at[k, d - 1], fwd_r.at[k, d - 1])

    def z_copy(d):
        return pltpu.make_async_remote_copy(
            src_ref=z_out.at[d - 1], dst_ref=z_in.at[d - 1],
            send_sem=z_s.at[d - 1], recv_sem=z_r.at[d - 1],
            device_id={"tp": lax.rem(rank + d, n_tp)}, device_id_type=MESH,
        )

    own_rows = pltpu.make_async_copy(tokens, rows_all.at[block(rank, slots)], tok_local)
    own_rows.start()

    barrier = pltpu.get_barrier_semaphore()
    for d in range(1, n_tp):
        pl.semaphore_signal(barrier, inc=1, device_id={"tp": lax.rem(rank + d, n_tp)}, device_id_type=MESH)
    for d in range(1, n_x):
        pl.semaphore_signal(barrier, inc=1, device_id={"dp": x_peer(d)}, device_id_type=MESH)
    pl.semaphore_signal(barrier, inc=1, device_id={"dp": sibling}, device_id_type=MESH)

    @pl.loop(0, n)
    def _(k):
        for copy in weight_copies(k):
            copy.start()

    pl.semaphore_wait(barrier, n_tp - 1 + n_x)
    for d in range(1, n_tp):
        token_copy(d).start()

    @pl.loop(0, n)
    def _(k):
        down_copy(k).start()

    product[...] = jnp.zeros_like(product)
    own_rows.wait()
    for d in range(1, n_tp):
        token_arrival(d).wait_recv()

    @pl.loop(0, n + 4)
    def _(k):
        @pl.when(k < n)
        def _():
            @pl.when(k >= SLOTS)
            def _():
                for i in range(n_x):
                    core_copy(k - SLOTS, i).wait_send()

            slot = lax.rem(k, SLOTS)
            first, second = weight_copies(k)
            first.wait()
            part[slot, 0] = jnp.dot(rows_all[...], gate_v[k], preferred_element_type=jnp.float32)
            second.wait()
            part[slot, 1] = jnp.dot(rows_all[...], up_v[k], preferred_element_type=jnp.float32)
            for i in range(n_x):
                core_copy(k, i).start()

        @pl.when((k >= 1) & (k <= n))
        def _():
            j = k - 1
            slot = lax.rem(j, SLOTS)
            for i in range(n_x):
                core_copy(j, i).wait_recv()
            for d in range(1, n_x):
                to = lax.rem(x + d, n_x)
                for g in range(2):
                    x_out[j, d - 1, g] = (
                        part[slot, g, block(to * 2 + core, share), :] + core_in[j, to, g]
                    ).astype(jnp.bfloat16)
                x_copy(j, d).start()
            for g in range(2):
                own[lax.rem(j, 2), g] = part[slot, g, block(dp, share), :] + core_in[j, x, g]

        @pl.when((k >= 2) & (k <= n + 1))
        def _():
            j = k - 2
            for d in range(1, n_x):
                x_copy(j, d).wait_recv()
            gate, up = own[lax.rem(j, 2), 0], own[lax.rem(j, 2), 1]
            for d in range(1, n_x):
                gate += x_in[j, d - 1, 0].astype(jnp.float32)
                up += x_in[j, d - 1, 1].astype(jnp.float32)
            hidden[j, block(dp, share), :] = (gate / (1.0 + jnp.exp(-gate)) * up).astype(jnp.bfloat16)
            for d in range(1, n_x):
                ag_copy(j, d).start()
            sib_copy(j).start()

        @pl.when((k >= 3) & (k <= n + 2))
        def _():
            j = k - 3
            for d in range(1, n_x):
                ag_arrival(j, d).wait_recv()
                fwd_copy(j, d).start()

        @pl.when(k >= 4)
        def _():
            j = k - 4
            sib_arrival(j).wait_recv()
            for d in range(1, n_x):
                fwd_arrival(j, d).wait_recv()
            down_copy(j).wait()
            product[...] += jnp.dot(hidden[j], down_v[j], preferred_element_type=jnp.float32)

    for d in range(1, n_tp):
        z_out[d - 1] = product[block(lax.rem(rank + d, n_tp), slots), :].astype(jnp.bfloat16)
        z_copy(d).start()

    for d in range(1, n_tp):
        token_copy(d).wait_send()

    @pl.loop(0, n)
    def _(k):
        @pl.when(k + SLOTS >= n)
        def _():
            for i in range(n_x):
                core_copy(k, i).wait_send()
        for d in range(1, n_x):
            x_copy(k, d).wait_send()
            ag_copy(k, d).wait_send()
            fwd_copy(k, d).wait_send()
        sib_copy(k).wait_send()

    total = product[block(rank, slots), :]
    for d in range(1, n_tp):
        z_copy(d).wait_recv()
        total += z_in[d - 1].astype(jnp.float32)
    out[...] = total.astype(jnp.bfloat16)
    for d in range(1, n_tp):
        z_copy(d).wait_send()


def solution(mesh):
    n_tp, n_dp = mesh.shape["tp"], mesh.shape["dp"]
    n_x = n_dp // 2

    def on_device(tokens, counts, gate_weight, up_weight, down_weight):
        slots, depth = tokens.shape
        units = gate_weight.shape[1]
        width = chunk_of(units)
        n = units // width
        rows = slots * n_tp
        share = rows // n_dp
        far = max(n_x - 1, 1)
        dma = pltpu.SemaphoreType.DMA
        mixed = pl.pallas_call(
            functools.partial(kernel, n_tp, n_dp, n, width),
            out_shape=jax.ShapeDtypeStruct((slots, depth), jnp.bfloat16),
            in_specs=[pl.BlockSpec(memory_space=pl.ANY)] * 4,
            out_specs=pl.BlockSpec(memory_space=pltpu.VMEM),
            scratch_shapes=[
                pltpu.VMEM((rows, depth), jnp.bfloat16),
                pltpu.VMEM((n, depth, width), jnp.bfloat16),
                pltpu.VMEM((n, depth, width), jnp.bfloat16),
                pltpu.VMEM((n, width, depth), jnp.bfloat16),
                pltpu.VMEM((SLOTS, 2, rows, width), jnp.float32),
                pltpu.VMEM((n, n_x, 2, share, width), jnp.float32),
                pltpu.VMEM((2, 2, share, width), jnp.float32),
                pltpu.VMEM((n, far, 2, share, width), jnp.bfloat16),
                pltpu.VMEM((n, far, 2, share, width), jnp.bfloat16),
                pltpu.VMEM((n, rows, width), jnp.bfloat16),
                pltpu.VMEM((rows, depth), jnp.float32),
                pltpu.VMEM((n_tp - 1, slots, depth), jnp.bfloat16),
                pltpu.VMEM((n_tp - 1, slots, depth), jnp.bfloat16),
                dma, dma((n_tp - 1,)), dma((n_tp - 1,)),
                dma((n,)), dma((n,)), dma((n,)),
                dma((n, n_x)), dma((n, n_x)), dma((n, far)), dma((n, far)),
                dma((n, far)), dma((n, far)), dma((n,)), dma((n,)), dma((n, far)), dma((n, far)),
                dma((n_tp - 1,)), dma((n_tp - 1,)),
            ],
            compiler_params=pltpu.CompilerParams(
                collective_id=0, has_side_effects=True, vmem_limit_bytes=62 * 1024 * 1024
            ),
        )(tokens, gate_weight, up_weight, down_weight)
        live = jnp.arange(slots, dtype=jnp.int32) < counts[0]
        return jnp.where(live[:, None], mixed, jnp.bfloat16(0.0))

    in_specs = (
        P(("groups", "tp"), "dp"),
        P(("groups", "tp")),
        P("dp", "tp"),
        P("dp", "tp"),
        P("tp", "dp"),
    )
    return jax.shard_map(
        on_device, mesh=mesh, in_specs=in_specs, out_specs=P(("groups", "tp"), "dp"), check_vma=False
    )
```

time: 151 us -> 59.8 us (0.40)
  waiting for transfers between devices: 91.9 us -> 0 us
  Pallas kernels: 0 us -> 56.8 us
  matrix products: 19.8 us -> 0 us
  blocking collectives: 17 us -> 0 us
  between operations: 13.8 us -> 0.67 us
  other arithmetic: 6.25 us -> 1.63 us
  local copies, waits for them, and re-layouts: 2.23 us -> 0 us
    reduce_scatter x2 -> x0, waiting for transfers between devices: 74.3 us -> none  [the longest x1 49.7 us: on_device(): shared = lax.psum_scatter(both, 'dp', scatter_dimension=0, tiled=True)]
    pallas_call x0 -> x1, Pallas kernels: none -> 56.8 us  [on_device(): pl.pallas_call(functools.partial(kernel, n_tp, n_dp, n, width), out_shape...]
    dot_general x3 -> x0, matrix products: 19.8 us -> none  [the longest x1 9.33 us: on_device(): jnp.dot(hidden, down_weight, preferred_element_type=jnp.float32)]
    all_gather x1 -> x0, waiting for transfers between devices: 17.6 us -> none  [on_device(): hidden = lax.all_gather(active, 'dp', axis=0, tiled=True)]
    all_gather x1 -> x0, blocking collectives: 17 us -> none  [on_device(): gathered = lax.all_gather(tokens, 'tp', axis=0, tiled=True)]
    convert_element_type x2 -> x0, other arithmetic: 3.8 us -> none  [the longest x1 2.14 us: on_device(): (jax.nn.silu(shared[:, :width]) * shared[:, width:]).astype(jnp.bfloat16)]
    concatenate x1 -> x0, other arithmetic: 2.44 us -> none  [on_device(): both = jnp.concatenate([gate_part, up_part], axis=1)]
    unnamed x2 -> x0, local copies, waits for them, and re-layouts: 2.23 us -> none
  transfers between devices with their start and end apart: 3 -> 0, of which waited for: 3 -> 0; matrix products, arithmetic and copies ran while one was open for 0% -> 0% of each run, Pallas kernels for 0% -> 0%
where the time goes in v1:
time: 59.8 us; the launch traced here: 59.1 us
  Pallas kernels  56.8 us (95%)
  other arithmetic  1.63 us (3%)
  between operations  0.67 us (1%)
    pallas_call x1, Pallas kernels, on_device(): pl.pallas_call(functools.partial(kernel, n_tp, n_dp, n, width), out_shape...  56.8 us
    select_n x1, other arithmetic, on_device(): return jnp.where(live[:, None], mixed, jnp.bfloat16(0.0))  1.62 us

profile of v1, /device:TPU:0, one launch (start us, length us, event | category | flops | bytes accessed | tf_op | source)
XLA Modules:
  0.0 59.1 jit_solution(10741900932870204835)
XLA Ops:
  0.7 56.8 %shard_map.55 = bf16[32,1792]{1,0:T(8,128)(2,1)} custom-call(bf16[32,1792]{1,0:T(8,128)(2,1)} %tokens.1, bf16[1792,4608]{1,0:T(8,128)(2,1)} %gate_w.1, bf16[1792,4608]{1,0:T(8,128)(2,1)} %up_w.1, bf16[4608,1792]{1,0:T(8,128)(2,1)} %down_w.1), custom_call_target="tpu_custom_call" | custom-call | tf_op jit(solution)/shard_map/pallas_call | solution.py:248
  57.5 1.6 %broadcast_select_fusion = bf16[32,1792]{1,0:T(8,128)(2,1)} fusion(bf16[32,1792]{1,0:T(8,128)(2,1)} %shard_map.55, pred[32]{0:T(512)(128)(4,1)S(1)} %iota_compare_fusion), kind=kLoop, calls=%fused_computation | loop fusion | flops 57344 | bytes 229408 | tf_op jit(solution)/shard_map/jit(_where)/select_n | solution.py:278
  (1 shorter events, 0.0 us)

commit v2 on v1

--- a/solution.py
+++ b/solution.py
@@ -8,11 +8,13 @@
 from jax.sharding import PartitionSpec as P
 
 MESH = pl.DeviceIdType.MESH
-SLOTS = 3
+SLOTS = 4
+LAG = 2
+HALVES = 2
 
 
 def chunk_of(units):
-    for width in (512, 384, 256, 128):
+    for width in (768, 512, 384, 256, 128):
         if units % width == 0:
             return width
     return units
@@ -30,8 +32,9 @@
     n_x = n_dp // 2
     x, core = lax.div(dp, 2), lax.rem(dp, 2)
     sibling = x * 2 + 1 - core
-    slots = tokens.shape[0]
+    slots = tokens.shape[0] // HALVES
     share = slots * n_tp // n_dp
+    steps = HALVES * n
 
     def x_peer(d):
         return lax.rem(x + d, n_x) * 2 + core
@@ -50,19 +53,18 @@
         rows = pl.ds(pl.multiple_of(k * width, width), width) if n > 1 else pl.ds(0, width)
         return pltpu.make_async_copy(down_w.at[rows, :], down_v.at[k], down_s.at[k])
 
-    def token_copy(d):
-        return pltpu.make_async_remote_copy(
-            src_ref=tokens, dst_ref=rows_all.at[block(rank, slots)],
-            send_sem=tok_s.at[d - 1], recv_sem=tok_r.at[d - 1],
+    def token_move(h, d, source):
+        return pltpu.make_async_remote_copy(
+            src_ref=tokens.at[pl.ds(h * slots, slots)], dst_ref=rows_all.at[h, block(source, slots)],
+            send_sem=tok_s.at[h, d - 1], recv_sem=tok_r.at[h, d - 1],
             device_id={"tp": lax.rem(rank + d, n_tp)}, device_id_type=MESH,
         )
 
-    def token_arrival(d):
-        return pltpu.make_async_remote_copy(
-            src_ref=tokens, dst_ref=rows_all.at[block(lax.rem(rank + n_tp - d, n_tp), slots)],
-            send_sem=tok_s.at[d - 1], recv_sem=tok_r.at[d - 1],
-            device_id={"tp": lax.rem(rank + d, n_tp)}, device_id_type=MESH,
-        )
+    def token_copy(h, d):
+        return token_move(h, d, rank)
+
+    def token_arrival(h, d):
+        return token_move(h, d, lax.rem(rank + n_tp - d, n_tp))
 
     def core_copy(k, i):
         return pltpu.make_async_remote_copy(
@@ -105,15 +107,26 @@
         owner = lax.rem(x + n_x - d, n_x) * 2 + 1 - core
         return hidden_copy(k, owner, sibling, fwd_s.at[k, d - 1], fwd_r.at[k, d - 1])
 
-    def z_copy(d):
-        return pltpu.make_async_remote_copy(
-            src_ref=z_out.at[d - 1], dst_ref=z_in.at[d - 1],
-            send_sem=z_s.at[d - 1], recv_sem=z_r.at[d - 1],
+    def z_copy(h, d):
+        return pltpu.make_async_remote_copy(
+            src_ref=z_out.at[h, d - 1], dst_ref=z_in.at[h, d - 1],
+            send_sem=z_s.at[h, d - 1], recv_sem=z_r.at[h, d - 1],
             device_id={"tp": lax.rem(rank + d, n_tp)}, device_id_type=MESH,
         )
 
-    own_rows = pltpu.make_async_copy(tokens, rows_all.at[block(rank, slots)], tok_local)
-    own_rows.start()
+    def send_product(h):
+        for d in range(1, n_tp):
+            z_out[h, d - 1] = product[h, block(lax.rem(rank + d, n_tp), slots), :].astype(jnp.bfloat16)
+            z_copy(h, d).start()
+
+    own_rows = [
+        pltpu.make_async_copy(
+            tokens.at[pl.ds(h * slots, slots)], rows_all.at[h, block(rank, slots)], tok_local.at[h]
+        )
+        for h in range(HALVES)
+    ]
+    for copy in own_rows:
+        copy.start()
 
     barrier = pltpu.get_barrier_semaphore()
     for d in range(1, n_tp):
@@ -129,38 +142,51 @@
 
     pl.semaphore_wait(barrier, n_tp - 1 + n_x)
     for d in range(1, n_tp):
-        token_copy(d).start()
+        token_copy(0, d).start()
 
     @pl.loop(0, n)
     def _(k):
         down_copy(k).start()
 
     product[...] = jnp.zeros_like(product)
-    own_rows.wait()
+    for copy in own_rows:
+        copy.wait()
     for d in range(1, n_tp):
-        token_arrival(d).wait_recv()
-
-    @pl.loop(0, n + 4)
+        token_arrival(0, d).wait_recv()
+    for h in range(1, HALVES):
+        for d in range(1, n_tp):
+            token_copy(h, d).start()
+
+    @pl.loop(0, steps + 4 * LAG)
     def _(k):
-        @pl.when(k < n)
+        @pl.when(k < steps)
         def _():
             @pl.when(k >= SLOTS)
             def _():
                 for i in range(n_x):
                     core_copy(k - SLOTS, i).wait_send()
 
-            slot = lax.rem(k, SLOTS)
-            first, second = weight_copies(k)
-            first.wait()
-            part[slot, 0] = jnp.dot(rows_all[...], gate_v[k], preferred_element_type=jnp.float32)
-            second.wait()
-            part[slot, 1] = jnp.dot(rows_all[...], up_v[k], preferred_element_type=jnp.float32)
+            for h in range(1, HALVES):
+                @pl.when(k == h * n)
+                def _():
+                    for d in range(1, n_tp):
+                        token_arrival(h, d).wait_recv()
+
+            slot, h, c = lax.rem(k, SLOTS), lax.div(k, n), lax.rem(k, n)
+
+            @pl.when(k < n)
+            def _():
+                for copy in weight_copies(c):
+                    copy.wait()
+
+            part[slot, 0] = jnp.dot(rows_all[h], gate_v[c], preferred_element_type=jnp.float32)
+            part[slot, 1] = jnp.dot(rows_all[h], up_v[c], preferred_element_type=jnp.float32)
             for i in range(n_x):
                 core_copy(k, i).start()
 
-        @pl.when((k >= 1) & (k <= n))
-        def _():
-            j = k - 1
+        @pl.when((k >= LAG) & (k < steps + LAG))
+        def _():
+            j = k - LAG
             slot = lax.rem(j, SLOTS)
             for i in range(n_x):
                 core_copy(j, i).wait_recv()
@@ -172,14 +198,14 @@
                     ).astype(jnp.bfloat16)
                 x_copy(j, d).start()
             for g in range(2):
-                own[lax.rem(j, 2), g] = part[slot, g, block(dp, share), :] + core_in[j, x, g]
-
-        @pl.when((k >= 2) & (k <= n + 1))
-        def _():
-            j = k - 2
+                own[lax.rem(j, LAG + 1), g] = part[slot, g, block(dp, share), :] + core_in[j, x, g]
+
+        @pl.when((k >= 2 * LAG) & (k < steps + 2 * LAG))
+        def _():
+            j = k - 2 * LAG
             for d in range(1, n_x):
                 x_copy(j, d).wait_recv()
-            gate, up = own[lax.rem(j, 2), 0], own[lax.rem(j, 2), 1]
+            gate, up = own[lax.rem(j, LAG + 1), 0], own[lax.rem(j, LAG + 1), 1]
             for d in range(1, n_x):
                 gate += x_in[j, d - 1, 0].astype(jnp.float32)
                 up += x_in[j, d - 1, 1].astype(jnp.float32)
@@ -188,32 +214,38 @@
                 ag_copy(j, d).start()
             sib_copy(j).start()
 
-        @pl.when((k >= 3) & (k <= n + 2))
-        def _():
-            j = k - 3
+        @pl.when((k >= 3 * LAG) & (k < steps + 3 * LAG))
+        def _():
+            j = k - 3 * LAG
             for d in range(1, n_x):
                 ag_arrival(j, d).wait_recv()
                 fwd_copy(j, d).start()
 
-        @pl.when(k >= 4)
-        def _():
-            j = k - 4
+        @pl.when(k >= 4 * LAG)
+        def _():
+            j = k - 4 * LAG
             sib_arrival(j).wait_recv()
             for d in range(1, n_x):
                 fwd_arrival(j, d).wait_recv()
-            down_copy(j).wait()
-            product[...] += jnp.dot(hidden[j], down_v[j], preferred_element_type=jnp.float32)
-
-    for d in range(1, n_tp):
-        z_out[d - 1] = product[block(lax.rem(rank + d, n_tp), slots), :].astype(jnp.bfloat16)
-        z_copy(d).start()
-
-    for d in range(1, n_tp):
-        token_copy(d).wait_send()
-
-    @pl.loop(0, n)
+            h, c = lax.div(j, n), lax.rem(j, n)
+
+            @pl.when(j < n)
+            def _():
+                down_copy(c).wait()
+
+            product[h] += jnp.dot(hidden[j], down_v[c], preferred_element_type=jnp.float32)
+            for h in range(HALVES):
+                @pl.when(j == h * n + n - 1)
+                def _():
+                    send_product(h)
+
+    for h in range(HALVES):
+        for d in range(1, n_tp):
+            token_copy(h, d).wait_send()
+
+    @pl.loop(0, steps)
     def _(k):
-        @pl.when(k + SLOTS >= n)
+        @pl.when(k + SLOTS >= steps)
         def _():
             for i in range(n_x):
                 core_copy(k, i).wait_send()
@@ -223,13 +255,15 @@
             fwd_copy(k, d).wait_send()
         sib_copy(k).wait_send()
 
-    total = product[block(rank, slots), :]
-    for d in range(1, n_tp):
-        z_copy(d).wait_recv()
-        total += z_in[d - 1].astype(jnp.float32)
-    out[...] = total.astype(jnp.bfloat16)
-    for d in range(1, n_tp):
-        z_copy(d).wait_send()
+    for h in range(HALVES):
+        total = product[h, block(rank, slots), :]
+        for d in range(1, n_tp):
+            z_copy(h, d).wait_recv()
+            total += z_in[h, d - 1].astype(jnp.float32)
+        out[pl.ds(h * slots, slots), :] = total.astype(jnp.bfloat16)
+    for h in range(HALVES):
+        for d in range(1, n_tp):
+            z_copy(h, d).wait_send()
 
 
 def solution(mesh):
@@ -241,7 +275,8 @@
         units = gate_weight.shape[1]
         width = chunk_of(units)
         n = units // width
-        rows = slots * n_tp
+        rows = slots * n_tp // HALVES
+        steps = HALVES * n
         share = rows // n_dp
         far = max(n_x - 1, 1)
         dma = pltpu.SemaphoreType.DMA
@@ -251,24 +286,25 @@
             in_specs=[pl.BlockSpec(memory_space=pl.ANY)] * 4,
             out_specs=pl.BlockSpec(memory_space=pltpu.VMEM),
             scratch_shapes=[
-                pltpu.VMEM((rows, depth), jnp.bfloat16),
+                pltpu.VMEM((HALVES, rows, depth), jnp.bfloat16),
                 pltpu.VMEM((n, depth, width), jnp.bfloat16),
                 pltpu.VMEM((n, depth, width), jnp.bfloat16),
                 pltpu.VMEM((n, width, depth), jnp.bfloat16),
                 pltpu.VMEM((SLOTS, 2, rows, width), jnp.float32),
-                pltpu.VMEM((n, n_x, 2, share, width), jnp.float32),
-                pltpu.VMEM((2, 2, share, width), jnp.float32),
-                pltpu.VMEM((n, far, 2, share, width), jnp.bfloat16),
-                pltpu.VMEM((n, far, 2, share, width), jnp.bfloat16),
-                pltpu.VMEM((n, rows, width), jnp.bfloat16),
-                pltpu.VMEM((rows, depth), jnp.float32),
-                pltpu.VMEM((n_tp - 1, slots, depth), jnp.bfloat16),
-                pltpu.VMEM((n_tp - 1, slots, depth), jnp.bfloat16),
-                dma, dma((n_tp - 1,)), dma((n_tp - 1,)),
+                pltpu.VMEM((steps, n_x, 2, share, width), jnp.float32),
+                pltpu.VMEM((LAG + 1, 2, share, width), jnp.float32),
+                pltpu.VMEM((steps, far, 2, share, width), jnp.bfloat16),
+                pltpu.VMEM((steps, far, 2, share, width), jnp.bfloat16),
+                pltpu.VMEM((steps, rows, width), jnp.bfloat16),
+                pltpu.VMEM((HALVES, rows, depth), jnp.float32),
+                pltpu.VMEM((HALVES, n_tp - 1, slots // HALVES, depth), jnp.bfloat16),
+                pltpu.VMEM((HALVES, n_tp - 1, slots // HALVES, depth), jnp.bfloat16),
+                dma((HALVES,)), dma((HALVES, n_tp - 1)), dma((HALVES, n_tp - 1)),
                 dma((n,)), dma((n,)), dma((n,)),
-                dma((n, n_x)), dma((n, n_x)), dma((n, far)), dma((n, far)),
-                dma((n, far)), dma((n, far)), dma((n,)), dma((n,)), dma((n, far)), dma((n, far)),
-                dma((n_tp - 1,)), dma((n_tp - 1,)),
+                dma((steps, n_x)), dma((steps, n_x)), dma((steps, far)), dma((steps, far)),
+                dma((steps, far)), dma((steps, far)), dma((steps,)), dma((steps,)),
+                dma((steps, far)), dma((steps, far)),
+                dma((HALVES, n_tp - 1)), dma((HALVES, n_tp - 1)),
             ],
             compiler_params=pltpu.CompilerParams(
                 collective_id=0, has_side_effects=True, vmem_limit_bytes=62 * 1024 * 1024

time: 59.8 us -> 50.4 us (0.84)
  Pallas kernels: 56.8 us -> 48 us
    pallas_call x1, Pallas kernels: 56.8 us -> 48 us  [on_device(): pl.pallas_call(functools.partial(kernel, n_tp, n_dp, n, width), out_shape...]
where the time goes in v2:
time: 50.4 us; the launch traced here: 50.3 us
  Pallas kernels  48 us (95%)
  other arithmetic  1.63 us (3%)
  between operations  0.67 us (1%)
    pallas_call x1, Pallas kernels, on_device(): pl.pallas_call(functools.partial(kernel, n_tp, n_dp, n, width), out_shape...  48 us
    select_n x1, other arithmetic, on_device(): return jnp.where(live[:, None], mixed, jnp.bfloat16(0.0))  1.62 us

profile of v2, /device:TPU:0, one launch (start us, length us, event | category | flops | bytes accessed | tf_op | source)
XLA Modules:
  0.0 50.3 jit_solution(9287661070774806384)
XLA Ops:
  0.7 48.0 %shard_map.55 = bf16[32,1792]{1,0:T(8,128)(2,1)} custom-call(bf16[32,1792]{1,0:T(8,128)(2,1)} %tokens.1, bf16[1792,4608]{1,0:T(8,128)(2,1)} %gate_w.1, bf16[1792,4608]{1,0:T(8,128)(2,1)} %up_w.1, bf16[4608,1792]{1,0:T(8,128)(2,1)} %down_w.1), custom_call_target="tpu_custom_call" | custom-call | tf_op jit(solution)/shard_map/pallas_call | solution.py:283
  48.6 1.6 %broadcast_select_fusion = bf16[32,1792]{1,0:T(8,128)(2,1)} fusion(bf16[32,1792]{1,0:T(8,128)(2,1)} %shard_map.55, pred[32]{0:T(512)(128)(4,1)S(1)} %iota_compare_fusion), kind=kLoop, calls=%fused_computation | loop fusion | flops 57344 | bytes 229408 | tf_op jit(solution)/shard_map/jit(_where)/select_n | solution.py:314
  (1 shorter events, 0.0 us)

commit v3 on v2

--- a/solution.py
+++ b/solution.py
@@ -9,7 +9,7 @@
 
 MESH = pl.DeviceIdType.MESH
 SLOTS = 4
-LAG = 2
+PAIR, ACT, FORWARD, DOWN = 1, 3, 5, 6
 HALVES = 2
 
 
@@ -157,7 +157,7 @@
         for d in range(1, n_tp):
             token_copy(h, d).start()
 
-    @pl.loop(0, steps + 4 * LAG)
+    @pl.loop(0, steps + DOWN)
     def _(k):
         @pl.when(k < steps)
         def _():
@@ -184,9 +184,9 @@
             for i in range(n_x):
                 core_copy(k, i).start()
 
-        @pl.when((k >= LAG) & (k < steps + LAG))
-        def _():
-            j = k - LAG
+        @pl.when((k >= PAIR) & (k < steps + PAIR))
+        def _():
+            j = k - PAIR
             slot = lax.rem(j, SLOTS)
             for i in range(n_x):
                 core_copy(j, i).wait_recv()
@@ -198,14 +198,14 @@
                     ).astype(jnp.bfloat16)
                 x_copy(j, d).start()
             for g in range(2):
-                own[lax.rem(j, LAG + 1), g] = part[slot, g, block(dp, share), :] + core_in[j, x, g]
-
-        @pl.when((k >= 2 * LAG) & (k < steps + 2 * LAG))
-        def _():
-            j = k - 2 * LAG
+                own[lax.rem(j, ACT - PAIR + 1), g] = part[slot, g, block(dp, share), :] + core_in[j, x, g]
+
+        @pl.when((k >= ACT) & (k < steps + ACT))
+        def _():
+            j = k - ACT
             for d in range(1, n_x):
                 x_copy(j, d).wait_recv()
-            gate, up = own[lax.rem(j, LAG + 1), 0], own[lax.rem(j, LAG + 1), 1]
+            gate, up = own[lax.rem(j, ACT - PAIR + 1), 0], own[lax.rem(j, ACT - PAIR + 1), 1]
             for d in range(1, n_x):
                 gate += x_in[j, d - 1, 0].astype(jnp.float32)
                 up += x_in[j, d - 1, 1].astype(jnp.float32)
@@ -214,16 +214,16 @@
                 ag_copy(j, d).start()
             sib_copy(j).start()
 
-        @pl.when((k >= 3 * LAG) & (k < steps + 3 * LAG))
-        def _():
-            j = k - 3 * LAG
+        @pl.when((k >= FORWARD) & (k < steps + FORWARD))
+        def _():
+            j = k - FORWARD
             for d in range(1, n_x):
                 ag_arrival(j, d).wait_recv()
                 fwd_copy(j, d).start()
 
-        @pl.when(k >= 4 * LAG)
-        def _():
-            j = k - 4 * LAG
+        @pl.when(k >= DOWN)
+        def _():
+            j = k - DOWN
             sib_arrival(j).wait_recv()
             for d in range(1, n_x):
                 fwd_arrival(j, d).wait_recv()
@@ -292,7 +292,7 @@
                 pltpu.VMEM((n, width, depth), jnp.bfloat16),
                 pltpu.VMEM((SLOTS, 2, rows, width), jnp.float32),
                 pltpu.VMEM((steps, n_x, 2, share, width), jnp.float32),
-                pltpu.VMEM((LAG + 1, 2, share, width), jnp.float32),
+                pltpu.VMEM((ACT - PAIR + 1, 2, share, width), jnp.float32),
                 pltpu.VMEM((steps, far, 2, share, width), jnp.bfloat16),
                 pltpu.VMEM((steps, far, 2, share, width), jnp.bfloat16),
                 pltpu.VMEM((steps, rows, width), jnp.bfloat16),

time: 50.4 us -> 49.7 us (0.986)
  Pallas kernels: 48 us -> 47.3 us
    pallas_call x1, Pallas kernels: 48 us -> 47.3 us  [on_device(): pl.pallas_call(functools.partial(kernel, n_tp, n_dp, n, width), out_shape...]
where the time goes in v3:
time: 49.7 us; the launch traced here: 49.6 us
  Pallas kernels  47.3 us (95%)
  other arithmetic  1.63 us (3%)
  between operations  0.67 us (1%)
    pallas_call x1, Pallas kernels, on_device(): pl.pallas_call(functools.partial(kernel, n_tp, n_dp, n, width), out_shape...  47.3 us
    select_n x1, other arithmetic, on_device(): return jnp.where(live[:, None], mixed, jnp.bfloat16(0.0))  1.62 us

profile of v3, /device:TPU:0, one launch (start us, length us, event | category | flops | bytes accessed | tf_op | source)
XLA Modules:
  0.0 49.6 jit_solution(4505424359810709475)
XLA Ops:
  0.7 47.3 %shard_map.55 = bf16[32,1792]{1,0:T(8,128)(2,1)} custom-call(bf16[32,1792]{1,0:T(8,128)(2,1)} %tokens.1, bf16[1792,4608]{1,0:T(8,128)(2,1)} %gate_w.1, bf16[1792,4608]{1,0:T(8,128)(2,1)} %up_w.1, bf16[4608,1792]{1,0:T(8,128)(2,1)} %down_w.1), custom_call_target="tpu_custom_call" | custom-call | tf_op jit(solution)/shard_map/pallas_call | solution.py:283
  48.0 1.6 %broadcast_select_fusion = bf16[32,1792]{1,0:T(8,128)(2,1)} fusion(bf16[32,1792]{1,0:T(8,128)(2,1)} %shard_map.55, pred[32]{0:T(512)(128)(4,1)S(1)} %iota_compare_fusion), kind=kLoop, calls=%fused_computation | loop fusion | flops 57344 | bytes 229408 | tf_op jit(solution)/shard_map/jit(_where)/select_n | solution.py:314
  (1 shorter events, 0.0 us)
